TPU v7x, 32 devices: a whole 2x2x4 slice. The times are simulated.
32 devices in a mesh: groups: 2 (over x), owner: 16 (over z, y, core).
Axes of the slice: x: 2, y: 2, z: 4, core: 2. Of those that a mesh axis runs over, the one named last changes fastest.
Arguments:
- features: bfloat16 [16384, 1024], P(('groups', 'owner')), parts along dimension 0, may hold values from -6 to 6
- history: bfloat16 [2, 32768, 1024], P(None, ('groups', 'owner')), parts along dimension 1, may hold values from -6 to 6
- weights: bfloat16 [2, 1024, 1024], replicated, may hold values from -0.1875 to 0.1875
- edge_weights: float32 [16384, 768], P(('groups', 'owner')), parts along dimension 0, may hold values from 0 to 10, as said below
- requests: int32 [32, 16, 16], P(('groups', 'owner')), parts along dimension 0, may hold values from 0 to 1023, as said below
- counts: int32 [32, 16], P(('groups', 'owner')), parts along dimension 0, may hold values from 1 to 16, as said below
- push_slots: int32 [32, 512], P(('groups', 'owner')), parts along dimension 0, may hold values from 0 to 1023, as said below
- cotangent: bfloat16 [16384, 1024], P(('groups', 'owner')), parts along dimension 0, may hold values from -6 to 6
Outputs:
- result: bfloat16 [16384, 1024], P(('groups', 'owner')), parts along dimension 0
- new_history: bfloat16 [1, 32768, 1024], P(None, ('groups', 'owner')), parts along dimension 1
- weight_grads: float32 [4, 1024, 1024], P('groups'), parts along dimension 0
There are 2 independent parts, one for each index of `groups`. A program takes and returns all parts, laid end to end along the dimension named above; an argument that names none is the same for every part. Nothing has to cross between parts.
Inputs may be any that keep to these rules, and one draw needn't show every extreme that they name: `requests`: every entry, padding slots too, names a row of that owner outside the rows in push_slots. `counts`: some owner has all 16 slots used by every device. `push_slots`: each owner's row holds distinct local rows. `edge_weights`: Nonnegative; the entry of each batch node's own column is positive.
All inputs are finite; a program needn't handle non-finite values.
Results may differ from a plain program's by a relative error of at most 0.0038.
The roundings to bfloat16 on the way count: a program that leaves them out, or rounds other values in their place, can miss the bound.
Values may be sent and summed in bfloat16 or wider, within the bound.
A program may use at most 128 MiB of HBM per device.

v0:
```python
import math

import jax
import jax.numpy as jnp
from jax import lax
from jax.sharding import PartitionSpec as P

RESIDUAL = 0.1


def strength(layer_no):
    return math.log(0.5 / (layer_no + 1) + 1.0)


def body(features, history, weights, edge_weights, requests, counts, push_slots, cotangent):
    owners = lax.axis_size("owner")
    batch_rows, hidden = features.shape
    layers = weights.shape[0]
    slot_count = requests.shape[2]
    push_rows = batch_rows // owners
    grad_scale = 1.0 / math.sqrt(owners * batch_rows)
    wanted = lax.all_to_all(requests, "owner", split_axis=1, concat_axis=0, tiled=True).reshape(
        owners * slot_count
    )
    valid_slots = (jnp.arange(slot_count, dtype=jnp.int32)[None, :] < counts[0][:, None]).reshape(
        owners * slot_count
    )
    valid_slots = jnp.concatenate(
        [jnp.ones((batch_rows,), jnp.float32), valid_slots.astype(jnp.float32)]
    )
    masked = edge_weights * valid_slots[None, :]
    norm_adj = (masked / jnp.sum(masked, axis=1, keepdims=True)).astype(jnp.bfloat16)
    self_adj = norm_adj[:, :batch_rows]
    far_adj = norm_adj[:, batch_rows:]
    start_float = features.astype(jnp.float32)
    current = features
    supports = []
    pre_list = []
    tables = []
    for layer_no in range(layers):
        mix_weight = strength(layer_no)
        served = history[layer_no][wanted].reshape(owners, slot_count, hidden)
        pulled = lax.all_to_all(served, "owner", split_axis=0, concat_axis=0, tiled=True).reshape(
            owners * slot_count, hidden
        )
        gathered_sum = jnp.dot(self_adj, current, preferred_element_type=jnp.float32)
        gathered_sum = gathered_sum + jnp.dot(far_adj, pulled, preferred_element_type=jnp.float32)
        support = ((1.0 - RESIDUAL) * gathered_sum + RESIDUAL * start_float).astype(jnp.bfloat16)
        linear_part = jnp.dot(support, weights[layer_no], preferred_element_type=jnp.float32)
        pre_relu = (1.0 - mix_weight) * support.astype(jnp.float32) + mix_weight * linear_part
        current = jnp.maximum(pre_relu, 0.0).astype(jnp.bfloat16)
        supports.append(support)
        pre_list.append(pre_relu)
        if layer_no + 1 < layers:
            outgoing = current.reshape(owners, push_rows, hidden)
            incoming = lax.all_to_all(
                outgoing, "owner", split_axis=0, concat_axis=0, tiled=True
            ).reshape(batch_rows, hidden)
            tables.append(history[layer_no + 1].at[push_slots[0]].set(incoming))
    weight_terms = [None] * layers
    upstream = cotangent.astype(jnp.float32)
    for layer_no in reversed(range(layers)):
        mix_weight = strength(layer_no)
        gate_grad = jnp.where(pre_list[layer_no] > 0, upstream, 0.0).astype(jnp.bfloat16)
        local_grad = (
            mix_weight
            * grad_scale
            * lax.dot_general(
                supports[layer_no],
                gate_grad,
                (((0,), (0,)), ((), ())),
                preferred_element_type=jnp.float32,
            )
        )
        weight_terms[layer_no] = local_grad
        if layer_no > 0:
            through_weight = lax.dot_general(
                gate_grad,
                weights[layer_no],
                (((1,), (1,)), ((), ())),
                preferred_element_type=jnp.float32,
            )
            support_grad = (
                (1.0 - mix_weight) * gate_grad.astype(jnp.float32) + mix_weight * through_weight
            ).astype(jnp.bfloat16)
            upstream = (1.0 - RESIDUAL) * lax.dot_general(
                self_adj, support_grad, (((0,), (0,)), ((), ())), preferred_element_type=jnp.float32
            )
    stacked = jnp.stack(weight_terms)
    stacked = lax.psum(stacked, "owner")
    return (current, jnp.stack(tables), stacked)


def solution(mesh):
    in_specs = (
        P(("groups", "owner"), None),
        P(None, ("groups", "owner"), None),
        P(),
        P(("groups", "owner"), None),
        P(("groups", "owner"), None, None),
        P(("groups", "owner"), None),
        P(("groups", "owner"), None),
        P(("groups", "owner"), None),
    )
    out_specs = (
        P(("groups", "owner"), None),
        P(None, ("groups", "owner"), None),
        P("groups", None, None),
    )
    return jax.shard_map(body, mesh=mesh, in_specs=in_specs, out_specs=out_specs, check_vma=False)
```

profile of v0, /device:TPU:1, one launch (start us, length us, event | category | flops | bytes accessed | tf_op | source)
XLA Modules:
  0.0 292.7 jit_solution(2948422967492267492)
XLA Ops:
  7.2 7.4 %all-to-all-start = ((s32[1,16,16]{2,0,1:T(1,128)}), s32[1,16,16]{2,0,1:T(1,128)S(1)}, u32[]{:S(2)}, u32[]{:S(2)}) async-start(s32[1,16,16]{2,0,1:T(1,128)} %bitcast.56), calls=%async_computation | async-start | bytes 16384 | tf_op jit(solution)/shard_map/all_to_all | solution.py:22
  14.5 4.0 %slice_bitcast_fusion = (bf16[1024,1024]{1,0:T(8,128)(2,1)S(1)}, bf16[1024,1024]{1,0:T(8,128)(2,1)}) fusion(bf16[2,1024,1024]{2,1,0:T(8,128)(2,1)} %param.9), kind=kLoop, calls=%fused_computation.18 | loop fusion | bytes 8388608 | tf_op jit(solution)/shard_map/squeeze | solution.py:42
  18.5 1.7 all-to-all-done
  21.5 4.2 %gather_fusion = bf16[256,1024]{1,0:T(8,128)(2,1)} fusion(bf16[1024,1024]{1,0:T(8,128)(2,1)} %get-tuple-element.4, s32[1024]{0:T(1024)S(1)} %pad_clamp_fusion), kind=kCustom, calls=%fused_computation | custom fusion | bytes 1049600 | tf_op jit(solution)/shard_map/gather | solution.py:42
  25.7 4.7 %all-to-all-start.1 = ((bf16[16,16,1024]{2,1,0:T(8,128)(2,1)}), bf16[16,16,1024]{2,1,0:T(8,128)(2,1)}, u32[]{:S(2)}, u32[]{:S(2)}) async-start(bf16[16,16,1024]{2,1,0:T(8,128)(2,1)} %bitcast.4), calls=%async_computation.1 | async-start | bytes 1048576 | tf_op jit(solution)/shard_map/all_to_all | solution.py:43
  34.9 2.0 fusion.20
  36.9 2.0 gather_fusion.1
  38.9 5.8 %all-to-all-done.1 = bf16[16,16,1024]{2,1,0:T(8,128)(2,1)} async-done(((bf16[16,16,1024]{2,1,0:T(8,128)(2,1)}), bf16[16,16,1024]{2,1,0:T(8,128)(2,1)}, u32[]{:S(2)}, u32[]{:S(2)}) %all-to-all-start.1) | async-done | bytes 524320 | tf_op jit(solution)/shard_map/all_to_all | solution.py:43
  44.7 4.5 %all-to-all-start.2 = ((bf16[16,16,1024]{2,1,0:T(8,128)(2,1)}), bf16[16,16,1024]{2,1,0:T(8,128)(2,1)}, u32[]{:S(2)}, u32[]{:S(2)}) async-start(bf16[16,16,1024]{2,1,0:T(8,128)(2,1)} %bitcast.54), calls=%async_computation.2 | async-start | bytes 1048576 | tf_op jit(solution)/shard_map/all_to_all | solution.py:43
  49.4 2.5 add_convert_fusion.2
  52.4 3.1 %maximum_convert_fusion.1 = (bf16[512,1024]{1,0:T(8,128)(2,1)}, f32[512,1024]{1,0:T(8,128)}) fusion(bf16[512,1024]{1,0:T(8,128)(2,1)S(1)} %add_convert_fusion.2, bf16[2,1024,1024]{2,1,0:T(8,128)(2,1)S(1)} %copy-done.11), kind=kOutput, calls=%fused_computation.19 | convolution fusion | flops 1076887552 | bytes 7340032 | tf_op jit(solution)/shard_map/dot_general | solution.py:49
  55.5 3.3 %fusion.18 = f32[512,1024]{1,0:T(8,128)} fusion(bf16[512,1024]{1,0:T(8,128)(2,1)} %get-tuple-element.5, bf16[512,768]{1,0:T(8,128)(2,1)S(1)} %copy-done.4), kind=kOutput, calls=%fused_computation.30 | convolution fusion | flops 536870912 | bytes 3670016 | tf_op jit(solution)/shard_map/dot_general | solution.py:46
  58.8 4.6 %all-to-all-done.2 = bf16[16,16,1024]{2,1,0:T(8,128)(2,1)} async-done(((bf16[16,16,1024]{2,1,0:T(8,128)(2,1)}), bf16[16,16,1024]{2,1,0:T(8,128)(2,1)}, u32[]{:S(2)}, u32[]{:S(2)}) %all-to-all-start.2) | async-done | bytes 524320 | tf_op jit(solution)/shard_map/all_to_all | solution.py:43
  63.4 2.5 add_convert_fusion.1
  66.5 2.3 maximum_convert_fusion
  68.8 3.3 %multiply_bitcast_fusion = f32[1,1024,1024]{2,1,0:T(8,128)} fusion(bf16[512,1024]{1,0:T(8,128)(2,1)S(1)} %add_convert_fusion.1, bf16[512,1024]{1,0:T(8,128)(2,1)S(1)} %copy-done.7, f32[512,1024]{1,0:T(8,128)S(1)} %get-tuple-element.8), kind=kOutput, calls=%fused_computation.4 | convolution fusion | flops 1076887552 | bytes 8388608 | tf_op jit(solution)/shard_map/dot_general | solution.py:68
  72.1 7.1 %select_convert_fusion = bf16[512,1024]{1,0:T(8,128)(2,1)} fusion(f32[512,1024]{1,0:T(8,128)} %get-tuple-element.6, bf16[2,1024,1024]{2,1,0:T(8,128)(2,1)} %param.10, bf16[512,768]{1,0:T(8,128)(2,1)S(1)} %copy-done.5, bf16[512,1024]{1,0:T(8,128)(2,1)} %param.15, f32[512,1024]{1,0:T(8,128)} %copy-done.6), kind=kOutput, calls=%fused_computation.12 | convolution fusion | flops 1619525632 | bytes 12058624 | tf_op jit(solution)/shard_map/dot_general | solution.py:86
  79.2 3.0 %multiply_bitcast_fusion.1 = f32[1,1024,1024]{2,1,0:T(8,128)S(1)} fusion(bf16[512,1024]{1,0:T(8,128)(2,1)} %copy-done.8, bf16[512,1024]{1,0:T(8,128)(2,1)} %select_convert_fusion), kind=kOutput, calls=%fused_computation.5 | convolution fusion | flops 1074790400 | bytes 6291456 | tf_op jit(solution)/shard_map/dot_general | solution.py:68
  82.2 4.2 %pad_maximum_fusion = f32[2,1024,1024]{2,1,0:T(8,128)} fusion(f32[1,1024,1024]{2,1,0:T(8,128)S(1)} %copy-done.1, f32[1,1024,1024]{2,1,0:T(8,128)S(1)} %multiply_bitcast_fusion.1), kind=kLoop, calls=%fused_computation.3 | loop fusion | flops 2097152 | bytes 16777216 | tf_op jit(solution)/shard_map/stack | solution.py:89
  86.5 4.4 %all-to-all-start.3 = ((bf16[16,32,1024]{2,1,0:T(8,128)(2,1)}), bf16[16,32,1024]{2,1,0:T(8,128)(2,1)S(1)}, u32[]{:S(2)}, u32[]{:S(2)}) async-start(bf16[16,32,1024]{2,1,0:T(8,128)(2,1)} %bitcast.13), calls=%async_computation.3 | async-start | bytes 2097152 | tf_op jit(solution)/shard_map/all_to_all | solution.py:56
  90.9 38.9 %all-to-all-done.3 = bf16[16,32,1024]{2,1,0:T(8,128)(2,1)S(1)} async-done(((bf16[16,32,1024]{2,1,0:T(8,128)(2,1)}), bf16[16,32,1024]{2,1,0:T(8,128)(2,1)S(1)}, u32[]{:S(2)}, u32[]{:S(2)}) %all-to-all-start.3) | async-done | bytes 1048608 | tf_op jit(solution)/shard_map/all_to_all | solution.py:56
  129.9 3.8 %scatter_fusion = bf16[1024,1024]{1,0:T(8,128)(2,1)S(1)} fusion(bf16[1024,1024]{1,0:T(8,128)(2,1)S(1)} %get-tuple-element.3, s32[512]{0:T(512)S(1)} %bitcast.55, bf16[512,1024]{1,0:T(8,128)(2,1)S(1)} %bitcast.53), kind=kCustom, calls=%fused_computation.2 | custom fusion | bytes 3147776 | tf_op jit(solution)/shard_map/scatter | solution.py:59
  133.7 143.6 %all-reduce.3.cloned.1.call-done = f32[2,1024,1024]{2,1,0:T(8,128)} async-done(((f32[2,1024,1024]{2,1,0:T(8,128)}), f32[2,1024,1024]{2,1,0:T(8,128)}) %all-reduce.3.cloned.1.call-update) | async-done | bytes 8388624 | tf_op jit(solution)/shard_map/psum | solution.py:90
  277.4 8.4 %copy.15 = f32[2,1024,1024]{2,1,0:T(8,128)} copy(f32[2,1024,1024]{2,1,0:T(8,128)} %all-reduce.3.cloned.1.call-done) | data formatting | bytes 16777216
  (39 shorter events, 7.0 us)
Async XLA Ops:
  7.2 13.1 %all-to-all-start = ((s32[1,16,16]{2,0,1:T(1,128)}), s32[1,16,16]{2,0,1:T(1,128)S(1)}, u32[]{:S(2)}, u32[]{:S(2)}) async-start(s32[1,16,16]{2,0,1:T(1,128)} %bitcast.56), calls=%async_computation | async-start | bytes 16384 | tf_op jit(solution)/shard_map/all_to_all | solution.py:22
  21.5 8.9 %copy-start.10 = (s32[1,16]{1,0:T(1,128)S(1)}, s32[1,16]{1,0:T(1,128)}, u32[]{:S(2)}) copy-start(s32[1,16]{1,0:T(1,128)} %param.13) | copy-start | bytes 196
  25.7 18.9 %all-to-all-start.1 = ((bf16[16,16,1024]{2,1,0:T(8,128)(2,1)}), bf16[16,16,1024]{2,1,0:T(8,128)(2,1)}, u32[]{:S(2)}, u32[]{:S(2)}) async-start(bf16[16,16,1024]{2,1,0:T(8,128)(2,1)} %bitcast.4), calls=%async_computation.1 | async-start | bytes 1048576 | tf_op jit(solution)/shard_map/all_to_all | solution.py:43
  30.4 4.4 %copy-start.2 = (bf16[512,1024]{1,0:T(8,128)(2,1)S(1)}, bf16[512,1024]{1,0:T(8,128)(2,1)}, u32[]{:S(2)}) copy-start(bf16[512,1024]{1,0:T(8,128)(2,1)} %param.8) | copy-start | bytes 3145732
  34.0 0.9 copy-start.3
  44.7 18.7 %all-to-all-start.2 = ((bf16[16,16,1024]{2,1,0:T(8,128)(2,1)}), bf16[16,16,1024]{2,1,0:T(8,128)(2,1)}, u32[]{:S(2)}, u32[]{:S(2)}) async-start(bf16[16,16,1024]{2,1,0:T(8,128)(2,1)} %bitcast.54), calls=%async_computation.2 | async-start | bytes 1048576 | tf_op jit(solution)/shard_map/all_to_all | solution.py:43
  49.2 228.2 %all-reduce.3.cloned.1.call-start = ((), (), s32[]{:S(2)}) async-start(), calls=%async_computation.4 | async-start | bytes 16777216 | tf_op jit(solution)/shard_map/psum | solution.py:90
  49.4 3.1 %copy-start.11 = (bf16[2,1024,1024]{2,1,0:T(8,128)(2,1)S(1)}, bf16[2,1024,1024]{2,1,0:T(8,128)(2,1)}, u32[]{:S(2)}) copy-start(bf16[2,1024,1024]{2,1,0:T(8,128)(2,1)} %param.10) | copy-start | bytes 12582916
  52.4 3.1 %copy-start.8 = (bf16[512,1024]{1,0:T(8,128)(2,1)}, bf16[512,1024]{1,0:T(8,128)(2,1)S(1)}, u32[]{:S(2)}) copy-start(bf16[512,1024]{1,0:T(8,128)(2,1)S(1)} %add_convert_fusion.2) | copy-start | bytes 3145732
  52.4 3.1 %copy-start.4 = (bf16[512,768]{1,0:T(8,128)(2,1)S(1)}, bf16[512,768]{1,0:T(8,128)(2,1)}, u32[]{:S(2)}) copy-start(bf16[512,768]{1,0:T(8,128)(2,1)} %copy-done.3) | copy-start | bytes 2359300
  63.4 3.1 %copy-start.12 = (bf16[2,1024,1024]{2,1,0:T(8,128)(2,1)S(1)}, bf16[2,1024,1024]{2,1,0:T(8,128)(2,1)}, u32[]{:S(2)}) copy-start(bf16[2,1024,1024]{2,1,0:T(8,128)(2,1)} %param.10) | copy-start | bytes 12582916
  66.5 2.3 copy-start.7
  68.8 3.3 %copy-start.6 = (f32[512,1024]{1,0:T(8,128)}, f32[512,1024]{1,0:T(8,128)S(1)}, u32[]{:S(2)}) copy-start(f32[512,1024]{1,0:T(8,128)S(1)} %get-tuple-element.8) | copy-start | bytes 6291460
  68.8 3.3 %copy-start.5 = (bf16[512,768]{1,0:T(8,128)(2,1)S(1)}, bf16[512,768]{1,0:T(8,128)(2,1)}, u32[]{:S(2)}) copy-start(bf16[512,768]{1,0:T(8,128)(2,1)} %copy-done.3) | copy-start | bytes 2359300
  79.2 3.0 %copy-start.1 = (f32[1,1024,1024]{2,1,0:T(8,128)S(1)}, f32[1,1024,1024]{2,1,0:T(8,128)}, u32[]{:S(2)}) copy-start(f32[1,1024,1024]{2,1,0:T(8,128)} %multiply_bitcast_fusion) | copy-start | bytes 12582916
  86.5 4.4 %copy-start.9 = (s32[1,512]{1,0:T(1,128)S(1)}, s32[1,512]{1,0:T(1,128)}, u32[]{:S(2)}) copy-start(s32[1,512]{1,0:T(1,128)} %param.14) | copy-start | bytes 6148
  86.5 43.4 %all-to-all-start.3 = ((bf16[16,32,1024]{2,1,0:T(8,128)(2,1)}), bf16[16,32,1024]{2,1,0:T(8,128)(2,1)S(1)}, u32[]{:S(2)}, u32[]{:S(2)}) async-start(bf16[16,32,1024]{2,1,0:T(8,128)(2,1)} %bitcast.13), calls=%async_computation.3 | async-start | bytes 2097152 | tf_op jit(solution)/shard_map/all_to_all | solution.py:56
  133.7 152.1 %copy-start = (bf16[1024,1024]{1,0:T(8,128)(2,1)}, bf16[1024,1024]{1,0:T(8,128)(2,1)S(1)}, u32[]{:S(2)}) copy-start(bf16[1024,1024]{1,0:T(8,128)(2,1)S(1)} %scatter_fusion) | copy-start | bytes 6291460
Sparse Core Ops, SparseCore 0:
  86.6 190.7 all-reduce.2
where the time goes:
time: 294 us; the launch traced here: 293 us
  waiting for transfers between devices  195 us (66%)
  matrix products  29.1 us (10%)
  local copies, waits for them, and re-layouts  25.1 us (9%)
  starting transfers between devices  21.2 us (7%)
  between operations  14.2 us (5%)
  other arithmetic  8.33 us (3%)
    psum x1, waiting for transfers between devices, body(): stacked = lax.psum(stacked, 'owner')  144 us
    all_to_all x1, waiting for transfers between devices, body(): lax.all_to_all(outgoing, 'owner', split_axis=0, concat_axis=0, tiled=True)  38.9 us
    unnamed x27, local copies, waits for them, and re-layouts  10.5 us
    all_to_all x2, waiting for transfers between devices, body(): lax.all_to_all(served, 'owner', split_axis=0, concat_axis=0, tiled=True)  10.4 us
    all_to_all x2, starting transfers between devices, body(): lax.all_to_all(served, 'owner', split_axis=0, concat_axis=0, tiled=True)  9.15 us
    all_to_all x1, starting transfers between devices, body(): lax.all_to_all(requests, 'owner', split_axis=1, concat_axis=0, tiled=True)  7.36 us
    dot_general x1, matrix products, body(): lax.dot_general(self_adj, support_grad, (((0,), (0,)), ((), ())), preferr...  7.08 us
    dot_general x2, matrix products, body(): lax.dot_general(supports[layer_no], gate_grad, (((0,), (0,)), ((), ())),...  6.3 us
  transfers between devices with their start and end apart: 5, of which 5 were waited for; matrix products, arithmetic and copies ran while one was open for 8% of the time, Pallas kernels for 0%

commit v1 on v0

v1 whole, which is shorter than its diff:
```python
import functools
import math

import jax
import jax.numpy as jnp
from jax import lax
from jax.experimental import pallas as pl
from jax.experimental.pallas import tpu as pltpu
from jax.sharding import PartitionSpec as P

RESIDUAL = 0.1
MESH = pl.DeviceIdType.MESH
TILE = 256
ROWS = 16
MIB = 1 << 20


def strength(layer_no):
    return math.log(0.5 / (layer_no + 1) + 1.0)


def ds(start, size, unit=ROWS):
    return pl.ds(pl.multiple_of(start, unit), size)


def dot(a, b, dims=((1,), (0,))):
    return lax.dot_general(a, b, (dims, ((), ())), preferred_element_type=jnp.float32)


def step_kernel(
    owners, slots, grad_scale,
    feat, hist, weights, edge, valid, req, cot,
    grads_out, incoming_out, result_out,
    req_in, onehot, served, pulled, adj, sup, gate, cur1, back, result, incoming,
    acc, sent, got, full,
    req_send, req_recv, pull_send, pull_recv, push_send, push_recv, ar_send, ar_recv, out_sem,
):
    me = lax.axis_index("owner")
    batch, hidden = feat.shape
    hist_rows = hist.shape[1]
    push = batch // owners
    steps = owners.bit_length() - 1
    size = ROWS * owners
    half = hidden // size
    chunks = 2 * half
    blocks = hidden // TILE

    barrier = pltpu.get_barrier_semaphore()

    def greet(p, c):
        pl.semaphore_signal(
            barrier, inc=1, device_id={"owner": lax.rem(me + p, owners)}, device_id_type=MESH
        )
        return c

    lax.fori_loop(1, owners, greet, 0)
    pl.semaphore_wait(barrier, owners - 1)

    def req_copy(p):
        peer = lax.rem(me + p, owners)
        return pltpu.make_async_remote_copy(
            src_ref=req.at[peer], dst_ref=req_in.at[me],
            send_sem=req_send.at[p], recv_sem=req_recv.at[p],
            device_id={"owner": peer}, device_id_type=MESH,
        )

    def each_peer(fn):
        def run(p, c):
            fn(p)
            return c

        lax.fori_loop(1, owners, run, 0)

    each_peer(lambda p: req_copy(p).start())
    req_in[me] = req[me]

    def norm_rows(i, c):
        rows = ds(i * 32, 32, 32)
        masked = edge[rows, :] * valid[...]
        adj[rows, :] = (masked / jnp.sum(masked, axis=1, keepdims=True)).astype(jnp.bfloat16)
        return c

    lax.fori_loop(0, batch // 32, norm_rows, 0)
    each_peer(lambda p: req_copy(p).wait())

    def pick_rows(o, c):
        rows = ds(o * slots, slots)
        want = req_in[o]
        for j in range(hist_rows // 128):
            lanes = lax.broadcasted_iota(jnp.int32, (slots, 128), 1) + j * 128
            onehot[rows, j * 128:(j + 1) * 128] = jnp.where(lanes == want, 1.0, 0.0).astype(
                jnp.bfloat16
            )
        return c

    lax.fori_loop(0, owners, pick_rows, 0)

    def pull_copy(layer_no, p):
        peer = lax.rem(me + p, owners)
        return pltpu.make_async_remote_copy(
            src_ref=served.at[layer_no, ds(peer * slots, slots)],
            dst_ref=pulled.at[layer_no, ds(me * slots, slots)],
            send_sem=pull_send.at[layer_no, p], recv_sem=pull_recv.at[layer_no, p],
            device_id={"owner": peer}, device_id_type=MESH,
        )

    for layer_no in range(2):
        def serve(j, c, layer_no=layer_no):
            cols = ds(j * TILE, TILE, TILE)
            served[layer_no, :, cols] = dot(onehot[...], hist[layer_no, :, cols]).astype(jnp.bfloat16)
            return c

        lax.fori_loop(0, blocks, serve, 0)
        each_peer(lambda p, layer_no=layer_no: pull_copy(layer_no, p).start())
        pulled[layer_no, ds(me * slots, slots), :] = served[layer_no, ds(me * slots, slots), :]

    def push_copy(p):
        peer = lax.rem(me + p, owners)
        return pltpu.make_async_remote_copy(
            src_ref=cur1.at[ds(peer * push, push)],
            dst_ref=incoming.at[ds(me * push, push)],
            send_sem=push_send.at[p], recv_sem=push_recv.at[p],
            device_id={"owner": peer}, device_id_type=MESH,
        )

    for layer_no in range(2):
        mix = strength(layer_no)
        source = feat if layer_no == 0 else cur1

        def own_sum(j, c, source=source):
            cols = ds(j * TILE, TILE, TILE)
            back[:, cols] = dot(adj[:, :batch], source[:, cols])
            return c

        lax.fori_loop(0, blocks, own_sum, 0)
        each_peer(lambda p, layer_no=layer_no: pull_copy(layer_no, p).wait())

        def far_sum(j, c, layer_no=layer_no):
            cols = ds(j * TILE, TILE, TILE)
            total = back[:, cols] + dot(adj[:, batch:], pulled[layer_no, :, cols])
            sup[layer_no, :, cols] = (
                (1.0 - RESIDUAL) * total + RESIDUAL * feat[:, cols].astype(jnp.float32)
            ).astype(jnp.bfloat16)
            return c

        lax.fori_loop(0, blocks, far_sum, 0)

        def linear(j, c, layer_no=layer_no, mix=mix):
            cols = ds(j * TILE, TILE, TILE)
            pre = (1.0 - mix) * sup[layer_no, :, cols].astype(jnp.float32) + mix * dot(
                sup[layer_no], weights[layer_no, :, cols]
            )
            out = jnp.maximum(pre, 0.0).astype(jnp.bfloat16)
            if layer_no == 0:
                cur1[:, cols] = out
            else:
                result[:, cols] = out
                gate[1, :, cols] = jnp.where(
                    pre > 0, cot[:, cols].astype(jnp.float32), 0.0
                ).astype(jnp.bfloat16)
            return c

        lax.fori_loop(0, blocks, linear, 0)
        if layer_no == 0:
            each_peer(lambda p: push_copy(p).start())
            incoming[ds(me * push, push), :] = cur1[ds(me * push, push), :]

    result_copy = pltpu.make_async_copy(result, result_out, out_sem.at[chunks])
    result_copy.start()

    def backward():
        mix = strength(1)

        def through(j, c):
            cols = ds(j * TILE, TILE, TILE)
            value = (1.0 - mix) * gate[1, :, cols].astype(jnp.float32) + mix * dot(
                gate[1], weights[1, cols, :], ((1,), (1,))
            )
            gate[0, :, cols] = value.astype(jnp.bfloat16)
            return c

        lax.fori_loop(0, blocks, through, 0)

        def up(j, c):
            cols = ds(j * TILE, TILE, TILE)
            upstream = (1.0 - RESIDUAL) * dot(adj[:, :batch], gate[0, :, cols], ((0,), (0,)))
            gate[0, :, cols] = jnp.where(
                cur1[:, cols].astype(jnp.float32) > 0, upstream, 0.0
            ).astype(jnp.bfloat16)
            return c

        lax.fori_loop(0, blocks, up, 0)

    bits = [lax.rem(me // (1 << b), 2) for b in range(steps)]
    peers = [me + (1 - 2 * bits[b]) * (1 << b) for b in range(steps)]
    width = [size >> (b + 1) for b in range(steps)]
    start = [0]
    for b in range(steps):
        start.append(start[-1] + bits[b] * width[b])
    other = [start[b] + (1 - bits[b]) * width[b] for b in range(steps)]
    stage_at = [size - (size >> b) for b in range(steps)]

    def rs_copy(k, b):
        rows = pl.ds(stage_at[b], width[b])
        return pltpu.make_async_remote_copy(
            src_ref=sent.at[k, rows], dst_ref=got.at[k, rows],
            send_sem=ar_send.at[k, b], recv_sem=ar_recv.at[k, b],
            device_id={"owner": peers[b]}, device_id_type=MESH,
        )

    def ag_copy(k, b):
        rows = ds(start[b + 1], width[b])
        return pltpu.make_async_remote_copy(
            src_ref=full.at[k, rows], dst_ref=full.at[k, rows],
            send_sem=ar_send.at[k, steps + b], recv_sem=ar_recv.at[k, steps + b],
            device_id={"owner": peers[b]}, device_id_type=MESH,
        )

    def out_copy(k):
        row = (1 - k // half) * hidden + lax.rem(k, half) * size
        return pltpu.make_async_copy(
            full.at[k], grads_out.at[ds(row, size)], out_sem.at[k]
        )

    def each_row(count, fn):
        def run(i, c):
            fn(i * ROWS)
            return c

        lax.fori_loop(0, count // ROWS, run, 0)

    def stage(k, s):
        if s == 0:
            @pl.when(k == half)
            def _():
                backward()

            layer_no = 1 - k // half
            scale = grad_scale * jnp.where(layer_no == 1, strength(1), strength(0))

            def product(i, c):
                cols = ds(lax.rem(k, half) * size + i * TILE, TILE, TILE)
                acc[k, ds(i * TILE, TILE, TILE), :] = scale * dot(
                    sup[layer_no, :, cols], gate[layer_no], ((0,), (0,))
                )
                return c

            lax.fori_loop(0, size // TILE, product, 0)

            def pack(i):
                sent[k, ds(i, ROWS), :] = acc[k, ds(other[0] + i, ROWS), :].astype(jnp.bfloat16)

            each_row(width[0], pack)
            rs_copy(k, 0).start()
        elif s < steps:
            rs_copy(k, s - 1).wait_recv()
            base = stage_at[s - 1]

            def pack(i):
                total = acc[k, ds(other[s] + i, ROWS), :] + got[
                    k, ds(base + (1 - bits[s]) * width[s] + i, ROWS), :
                ].astype(jnp.float32)
                sent[k, ds(stage_at[s] + i, ROWS), :] = total.astype(jnp.bfloat16)

            each_row(width[s], pack)
            rs_copy(k, s).start()

            def keep(i):
                rows = ds(start[s + 1] + i, ROWS)
                acc[k, rows, :] = acc[k, rows, :] + got[
                    k, ds(base + bits[s] * width[s] + i, ROWS), :
                ].astype(jnp.float32)

            each_row(width[s], keep)
        elif s == steps:
            rs_copy(k, s - 1).wait_recv()
            rows = ds(start[steps], ROWS)
            full[k, rows, :] = (
                acc[k, rows, :] + got[k, pl.ds(stage_at[steps - 1], ROWS), :].astype(jnp.float32)
            ).astype(jnp.bfloat16)
            ag_copy(k, steps - 1).start()
        else:
            b = 2 * steps - s
            rows = ds(other[b], width[b])
            pltpu.make_async_remote_copy(
                src_ref=full.at[k, rows], dst_ref=full.at[k, rows],
                send_sem=ar_send.at[k, steps + b], recv_sem=ar_recv.at[k, steps + b],
                device_id={"owner": peers[b]}, device_id_type=MESH,
            ).wait_recv()
            if b > 0:
                ag_copy(k, b - 1).start()
            else:
                out_copy(k).start()

    def turn(t, c):
        for s in range(2 * steps, -1, -1):
            k = t - s

            @pl.when((k >= 0) & (k < chunks))
            def _(k=k, s=s):
                stage(k, s)

        return c

    lax.fori_loop(0, chunks + 2 * steps, turn, 0)

    each_peer(lambda p: push_copy(p).wait())
    incoming_copy = pltpu.make_async_copy(incoming, incoming_out, out_sem.at[chunks + 1])
    incoming_copy.start()

    def drain(k, c):
        for b in range(steps):
            rs_copy(k, b).wait_send()
            ag_copy(k, b).wait_send()
        out_copy(k).wait()
        return c

    lax.fori_loop(0, chunks, drain, 0)
    result_copy.wait()
    incoming_copy.wait()


def finish_kernel(grads, incoming, hist, slots, result, grads_out, table_out, result_out):
    grads_out[...] = grads[...].astype(jnp.float32)
    result_out[...] = result[...]
    rows = table_out.shape[1]
    first = pl.program_id(0) * rows
    row_ids = lax.broadcasted_iota(jnp.int32, (rows, slots.shape[1]), 0) + first
    hit = row_ids == slots[...]
    place = jnp.where(hit, 1.0, 0.0)
    fresh = dot(place.astype(jnp.bfloat16), incoming[...])
    used = jnp.max(place, axis=1, keepdims=True)
    table_out[0] = jnp.where(used > 0, fresh, hist[0].astype(jnp.float32)).astype(jnp.bfloat16)


def body(features, history, weights, edge_weights, requests, counts, push_slots, cotangent):
    owners = lax.axis_size("owner")
    batch, hidden = features.shape
    layers, hist_rows, _ = history.shape
    slots = requests.shape[2]
    cells = owners * slots
    columns = batch + cells
    steps = owners.bit_length() - 1
    size = ROWS * owners
    chunks = layers * hidden // size
    grad_scale = 1.0 / math.sqrt(owners * batch)
    req = jnp.broadcast_to(requests[0][:, :, None], (owners, slots, 128))
    used = (jnp.arange(slots, dtype=jnp.int32)[None, :] < counts[0][:, None]).reshape(1, cells)
    valid = jnp.concatenate([jnp.ones((1, batch), jnp.float32), used.astype(jnp.float32)], axis=1)
    bf = jnp.bfloat16
    vmem = pl.BlockSpec(memory_space=pltpu.VMEM)
    hbm = pl.BlockSpec(memory_space=pl.ANY)
    dma = pltpu.SemaphoreType.DMA
    grads, incoming, result = pl.pallas_call(
        functools.partial(step_kernel, owners, slots, grad_scale),
        out_shape=(
            jax.ShapeDtypeStruct((layers * hidden, hidden), bf),
            jax.ShapeDtypeStruct((batch, hidden), bf),
            jax.ShapeDtypeStruct((batch, hidden), bf),
        ),
        in_specs=[vmem] * 7,
        out_specs=(hbm, hbm, hbm),
        scratch_shapes=[
            pltpu.VMEM((owners, slots, 128), jnp.int32),
            pltpu.VMEM((cells, hist_rows), bf),
            pltpu.VMEM((2, cells, hidden), bf),
            pltpu.VMEM((2, cells, hidden), bf),
            pltpu.VMEM((batch, columns), bf),
            pltpu.VMEM((2, batch, hidden), bf),
            pltpu.VMEM((2, batch, hidden), bf),
            pltpu.VMEM((batch, hidden), bf),
            pltpu.VMEM((batch, hidden), jnp.float32),
            pltpu.VMEM((batch, hidden), bf),
            pltpu.VMEM((batch, hidden), bf),
            pltpu.VMEM((chunks, size, hidden), jnp.float32),
            pltpu.VMEM((chunks, size, hidden), bf),
            pltpu.VMEM((chunks, size, hidden), bf),
            pltpu.VMEM((chunks, size, hidden), bf),
            dma((owners,)), dma((owners,)),
            dma((2, owners)), dma((2, owners)),
            dma((owners,)), dma((owners,)),
            dma((chunks, 2 * steps)), dma((chunks, 2 * steps)),
            dma((chunks + 2,)),
        ],
        compiler_params=pltpu.CompilerParams(
            collective_id=0, has_side_effects=True, vmem_limit_bytes=60 * MIB
        ),
    )(features, history, weights, edge_weights, valid, req, cotangent)

    parts = 8
    table_rows = hist_rows // parts
    grad_rows = layers * hidden // parts
    out_grads, table, out = pl.pallas_call(
        finish_kernel,
        grid=(parts,),
        out_shape=(
            jax.ShapeDtypeStruct((layers * hidden, hidden), jnp.float32),
            jax.ShapeDtypeStruct((1, hist_rows, hidden), bf),
            jax.ShapeDtypeStruct((batch, hidden), bf),
        ),
        in_specs=[
            pl.BlockSpec((grad_rows, hidden), lambda i: (i, 0)),
            pl.BlockSpec((batch, hidden), lambda i: (0, 0)),
            pl.BlockSpec((1, table_rows, hidden), lambda i: (1, i, 0)),
            pl.BlockSpec((1, batch), lambda i: (0, 0)),
            pl.BlockSpec((batch // parts, hidden), lambda i: (i, 0)),
        ],
        out_specs=(
            pl.BlockSpec((grad_rows, hidden), lambda i: (i, 0)),
            pl.BlockSpec((1, table_rows, hidden), lambda i: (0, i, 0)),
            pl.BlockSpec((batch // parts, hidden), lambda i: (i, 0)),
        ),
        compiler_params=pltpu.CompilerParams(vmem_limit_bytes=32 * MIB),
    )(grads, incoming, history, push_slots, result)
    return out, table, out_grads.reshape(layers, hidden, hidden)


def solution(mesh):
    in_specs = (
        P(("groups", "owner"), None),
        P(None, ("groups", "owner"), None),
        P(),
        P(("groups", "owner"), None),
        P(("groups", "owner"), None, None),
        P(("groups", "owner"), None),
        P(("groups", "owner"), None),
        P(("groups", "owner"), None),
    )
    out_specs = (
        P(("groups", "owner"), None),
        P(None, ("groups", "owner"), None),
        P("groups", None, None),
    )
    return jax.shard_map(body, mesh=mesh, in_specs=in_specs, out_specs=out_specs, check_vma=False)
```

time: 294 us -> 141 us (0.48)
  waiting for transfers between devices: 195 us -> 0 us
  Pallas kernels: 0 us -> 131 us
  matrix products: 29.1 us -> 0 us
  starting transfers between devices: 21.2 us -> 0 us
  local copies, waits for them, and re-layouts: 25.1 us -> 8.36 us
  between operations: 14.2 us -> 0.66 us
  other arithmetic: 8.33 us -> 1.32 us
    psum x1 -> x0, waiting for transfers between devices: 144 us -> none  [body(): stacked = lax.psum(stacked, 'owner')]
    pallas_call x0 -> x2, Pallas kernels: none -> 131 us  [the longest x1 125 us: body(): pl.pallas_call(functools.partial(step_kernel, owners, slots, grad_scale),...]
    all_to_all x4 -> x0, waiting for transfers between devices: 51.1 us -> none  [the longest x1 38.9 us: body(): lax.all_to_all(outgoing, 'owner', split_axis=0, concat_axis=0, tiled=True)]
    dot_general x9 -> x0, matrix products: 29.1 us -> none  [the longest x1 7.08 us: body(): lax.dot_general(self_adj, support_grad, (((0,), (0,)), ((), ())), preferr...]
    all_to_all x4 -> x0, starting transfers between devices: 20.9 us -> none  [the longest x2 9.15 us: body(): lax.all_to_all(served, 'owner', split_axis=0, concat_axis=0, tiled=True)]
    gather x2 -> x0, local copies, waits for them, and re-layouts: 6.18 us -> none  [body(): served = history[layer_no][wanted].reshape(owners, slot_count, hidden)]
    another operation x1 -> x0, other arithmetic: 4.24 us -> none  [body(): stacked = jnp.stack(weight_terms)]
    squeeze x1 -> x0, local copies, waits for them, and re-layouts: 3.98 us -> none  [body(): served = history[layer_no][wanted].reshape(owners, slot_count, hidden)]
  transfers between devices with their start and end apart: 5 -> 0, of which waited for: 5 -> 0; matrix products, arithmetic and copies ran while one was open for 8% -> 0% of each run, Pallas kernels for 0% -> 0%
where the time goes in v1:
time: 141 us
  Pallas kernels  131 us (93%)
  local copies, waits for them, and re-layouts  8.36 us (6%)
    pallas_call x1, Pallas kernels, body(): pl.pallas_call(functools.partial(step_kernel, owners, slots, grad_scale),...  125 us
    unnamed x10, local copies, waits for them, and re-layouts  6.82 us
    pallas_call x1, Pallas kernels, body(): pl.pallas_call(finish_kernel, grid=(parts,), out_shape=(jax.ShapeDtypeStr...  5.98 us

profile of v1, /device:TPU:1, one launch (start us, length us, event | category | flops | bytes accessed | tf_op | source)
XLA Modules:
  0.0 141.1 jit_solution(7258024877338107092)
XLA Ops:
  0.6 0.7 iota_compare_fusion
  1.4 0.1 convert_element_type.12
  1.4 0.6 pad_convert_fusion.valid
  2.0 1.5 %broadcast_in_dim.10.req = s32[16,16,128]{2,1,0:T(8,128)} broadcast(s32[16,16]{1,0:T(8,128)} %bitcast.3), dimensions={0,1} | broadcast | bytes 132096 | tf_op jit(solution)/shard_map/broadcast_in_dim | solution.py:347
  3.5 0.0 copy-start.4
  3.5 124.8 %shard_map.103 = (bf16[2048,1024]{1,0:T(8,128)(2,1)}, bf16[512,1024]{1,0:T(8,128)(2,1)}, bf16[512,1024]{1,0:T(8,128)(2,1)}) custom-call(bf16[512,1024]{1,0:T(8,128)(2,1)} %feat.1, bf16[2,1024,1024]{2,1,0:T(8,128)(2,1)} %hist.3, bf16[2,1024,1024]{2,1,0:T(8,128)(2,1)} %weights.1, f32[512,768]{1,0:T(8,128)} %edge.1, f32[1,768]{1,0:T(1,128)} %pad_convert_fusion.valid, ...), custom_call_target="tpu_custom_call" | custom-call | tf_op jit(solution)/shard_map/pallas_call | solution.py:354
  128.3 0.0 copy-done.4
  128.3 0.0 copy-start
  128.3 2.2 %copy-done = bf16[2,1024,1024]{2,1,0:T(8,128)(2,1)S(1)} copy-done((bf16[2,1024,1024]{2,1,0:T(8,128)(2,1)S(1)}, bf16[2,1024,1024]{2,1,0:T(8,128)(2,1)}, u32[]{:S(2)}) %copy-start) | copy-done | bytes 4194328
  130.5 0.0 copy-start.1
  130.5 2.2 %copy-done.1 = bf16[2048,1024]{1,0:T(8,128)(2,1)S(1)} copy-done((bf16[2048,1024]{1,0:T(8,128)(2,1)S(1)}, bf16[2048,1024]{1,0:T(8,128)(2,1)}, u32[]{:S(2)}) %copy-start.1) | copy-done | bytes 4194328
  132.7 0.0 copy-start.2
  132.7 1.2 copy-done.2
  133.9 0.0 copy-start.3
  133.9 1.2 copy-done.3
  135.1 6.0 %shard_map.104 = (f32[2048,1024]{1,0:T(8,128)}, bf16[1,1024,1024]{2,1,0:T(8,128)(2,1)}, bf16[512,1024]{1,0:T(8,128)(2,1)}) custom-call(bf16[2048,1024]{1,0:T(8,128)(2,1)S(1)} %copy-done.1, bf16[512,1024]{1,0:T(8,128)(2,1)S(1)} %copy-done.2, bf16[2,1024,1024]{2,1,0:T(8,128)(2,1)S(1)} %copy-done, s32[1,512]{1,0:T(1,128)S(1)} %copy-done.4, ...), custom_call_target="tpu_custom_call" | custom-call | tf_op jit(solution)/shard_map/pallas_call | solution.py:393
Async XLA Ops:
  3.5 124.8 %copy-start.4 = (s32[1,512]{1,0:T(1,128)S(1)}, s32[1,512]{1,0:T(1,128)}, u32[]{:S(2)}) copy-start(s32[1,512]{1,0:T(1,128)} %slots.1) | copy-start | bytes 6148
  128.3 2.2 %copy-start = (bf16[2,1024,1024]{2,1,0:T(8,128)(2,1)S(1)}, bf16[2,1024,1024]{2,1,0:T(8,128)(2,1)}, u32[]{:S(2)}) copy-start(bf16[2,1024,1024]{2,1,0:T(8,128)(2,1)} %hist.3) | copy-start | bytes 12582916
  130.5 2.2 %copy-start.1 = (bf16[2048,1024]{1,0:T(8,128)(2,1)S(1)}, bf16[2048,1024]{1,0:T(8,128)(2,1)}, u32[]{:S(2)}) copy-start(bf16[2048,1024]{1,0:T(8,128)(2,1)} %get-tuple-element.9.grads) | copy-start | bytes 12582916
  132.7 1.2 copy-start.2
  133.9 1.2 copy-start.3

commit v2 on v1

--- a/solution.py
+++ b/solution.py
@@ -12,6 +12,8 @@
 MESH = pl.DeviceIdType.MESH
 TILE = 256
 ROWS = 16
+SPLIT = 1
+GAP = 2
 MIB = 1 << 20
 
 
@@ -29,11 +31,11 @@
 
 def step_kernel(
     owners, slots, grad_scale,
-    feat, hist, weights, edge, valid, req, cot,
+    feat_in, hist_in, weights_in, edge_in, valid, req, cot_in,
     grads_out, incoming_out, result_out,
-    req_in, onehot, served, pulled, adj, sup, gate, cur1, back, result, incoming,
+    feat, hist, weights, edge, cot, req_in, onehot, served, pulled, adj, sup, gate, cur1, back, result, incoming,
     acc, sent, got, full,
-    req_send, req_recv, pull_send, pull_recv, push_send, push_recv, ar_send, ar_recv, out_sem,
+    req_send, req_recv, pull_send, pull_recv, push_send, push_recv, ar_send, ar_recv, out_sem, in_sem,
 ):
     me = lax.axis_index("owner")
     batch, hidden = feat.shape
@@ -41,9 +43,20 @@
     push = batch // owners
     steps = owners.bit_length() - 1
     size = ROWS * owners
-    half = hidden // size
+    wide = hidden // SPLIT
+    half = SPLIT * hidden // size
     chunks = 2 * half
     blocks = hidden // TILE
+
+    loads = {}
+    for i, (name, src, dst) in enumerate((
+        ("edge", edge_in, edge), ("hist0", hist_in.at[0], hist.at[0]),
+        ("hist1", hist_in.at[1], hist.at[1]), ("feat", feat_in, feat),
+        ("weights0", weights_in.at[0], weights.at[0]),
+        ("weights1", weights_in.at[1], weights.at[1]), ("cot", cot_in, cot),
+    )):
+        loads[name] = pltpu.make_async_copy(src, dst, in_sem.at[i])
+        loads[name].start()
 
     barrier = pltpu.get_barrier_semaphore()
 
@@ -73,6 +86,8 @@
 
     each_peer(lambda p: req_copy(p).start())
     req_in[me] = req[me]
+
+    loads["edge"].wait()
 
     def norm_rows(i, c):
         rows = ds(i * 32, 32, 32)
@@ -104,15 +119,20 @@
             device_id={"owner": peer}, device_id_type=MESH,
         )
 
-    for layer_no in range(2):
-        def serve(j, c, layer_no=layer_no):
+    def serve(layer_no):
+        loads[f"hist{layer_no}"].wait()
+
+        def pick(j, c):
             cols = ds(j * TILE, TILE, TILE)
             served[layer_no, :, cols] = dot(onehot[...], hist[layer_no, :, cols]).astype(jnp.bfloat16)
             return c
 
-        lax.fori_loop(0, blocks, serve, 0)
-        each_peer(lambda p, layer_no=layer_no: pull_copy(layer_no, p).start())
+        lax.fori_loop(0, blocks, pick, 0)
         pulled[layer_no, ds(me * slots, slots), :] = served[layer_no, ds(me * slots, slots), :]
+
+    serve(0)
+    each_peer(lambda p: pull_copy(0, p).start())
+    serve(1)
 
     def push_copy(p):
         peer = lax.rem(me + p, owners)
@@ -126,6 +146,8 @@
     for layer_no in range(2):
         mix = strength(layer_no)
         source = feat if layer_no == 0 else cur1
+        if layer_no == 0:
+            loads["feat"].wait()
 
         def own_sum(j, c, source=source):
             cols = ds(j * TILE, TILE, TILE)
@@ -134,6 +156,10 @@
 
         lax.fori_loop(0, blocks, own_sum, 0)
         each_peer(lambda p, layer_no=layer_no: pull_copy(layer_no, p).wait())
+        if layer_no == 0:
+            each_peer(lambda p: pull_copy(1, p).start())
+        else:
+            each_peer(lambda p: push_copy(p).start())
 
         def far_sum(j, c, layer_no=layer_no):
             cols = ds(j * TILE, TILE, TILE)
@@ -144,6 +170,9 @@
             return c
 
         lax.fori_loop(0, blocks, far_sum, 0)
+        loads[f"weights{layer_no}"].wait()
+        if layer_no == 1:
+            loads["cot"].wait()
 
         def linear(j, c, layer_no=layer_no, mix=mix):
             cols = ds(j * TILE, TILE, TILE)
@@ -162,7 +191,6 @@
 
         lax.fori_loop(0, blocks, linear, 0)
         if layer_no == 0:
-            each_peer(lambda p: push_copy(p).start())
             incoming[ds(me * push, push), :] = cur1[ds(me * push, push), :]
 
     result_copy = pltpu.make_async_copy(result, result_out, out_sem.at[chunks])
@@ -217,9 +245,10 @@
         )
 
     def out_copy(k):
-        row = (1 - k // half) * hidden + lax.rem(k, half) * size
+        row = (1 - k // half) * hidden + lax.rem(k, half) // SPLIT * size
+        cols = ds(lax.rem(k, SPLIT) * wide, wide, 128)
         return pltpu.make_async_copy(
-            full.at[k], grads_out.at[ds(row, size)], out_sem.at[k]
+            full.at[k], grads_out.at[ds(row, size), cols], out_sem.at[k]
         )
 
     def each_row(count, fn):
@@ -239,9 +268,10 @@
             scale = grad_scale * jnp.where(layer_no == 1, strength(1), strength(0))
 
             def product(i, c):
-                cols = ds(lax.rem(k, half) * size + i * TILE, TILE, TILE)
+                rows = ds(lax.rem(k, half) // SPLIT * size + i * TILE, TILE, TILE)
+                cols = ds(lax.rem(k, SPLIT) * wide, wide, 128)
                 acc[k, ds(i * TILE, TILE, TILE), :] = scale * dot(
-                    sup[layer_no, :, cols], gate[layer_no], ((0,), (0,))
+                    sup[layer_no, :, rows], gate[layer_no, :, cols], ((0,), (0,))
                 )
                 return c
 
@@ -294,7 +324,7 @@
 
     def turn(t, c):
         for s in range(2 * steps, -1, -1):
-            k = t - s
+            k = t - GAP * s
 
             @pl.when((k >= 0) & (k < chunks))
             def _(k=k, s=s):
@@ -302,7 +332,7 @@
 
         return c
 
-    lax.fori_loop(0, chunks + 2 * steps, turn, 0)
+    lax.fori_loop(0, chunks + GAP * 2 * steps, turn, 0)
 
     each_peer(lambda p: push_copy(p).wait())
     incoming_copy = pltpu.make_async_copy(incoming, incoming_out, out_sem.at[chunks + 1])
@@ -342,7 +372,8 @@
     columns = batch + cells
     steps = owners.bit_length() - 1
     size = ROWS * owners
-    chunks = layers * hidden // size
+    chunks = SPLIT * layers * hidden // size
+    wide = hidden // SPLIT
     grad_scale = 1.0 / math.sqrt(owners * batch)
     req = jnp.broadcast_to(requests[0][:, :, None], (owners, slots, 128))
     used = (jnp.arange(slots, dtype=jnp.int32)[None, :] < counts[0][:, None]).reshape(1, cells)
@@ -358,9 +389,14 @@
             jax.ShapeDtypeStruct((batch, hidden), bf),
             jax.ShapeDtypeStruct((batch, hidden), bf),
         ),
-        in_specs=[vmem] * 7,
+        in_specs=[hbm] * 4 + [vmem] * 2 + [hbm],
         out_specs=(hbm, hbm, hbm),
         scratch_shapes=[
+            pltpu.VMEM((batch, hidden), bf),
+            pltpu.VMEM((layers, hist_rows, hidden), bf),
+            pltpu.VMEM((layers, hidden, hidden), bf),
+            pltpu.VMEM((batch, columns), jnp.float32),
+            pltpu.VMEM((batch, hidden), bf),
             pltpu.VMEM((owners, slots, 128), jnp.int32),
             pltpu.VMEM((cells, hist_rows), bf),
             pltpu.VMEM((2, cells, hidden), bf),
@@ -372,22 +408,23 @@
             pltpu.VMEM((batch, hidden), jnp.float32),
             pltpu.VMEM((batch, hidden), bf),
             pltpu.VMEM((batch, hidden), bf),
-            pltpu.VMEM((chunks, size, hidden), jnp.float32),
-            pltpu.VMEM((chunks, size, hidden), bf),
-            pltpu.VMEM((chunks, size, hidden), bf),
-            pltpu.VMEM((chunks, size, hidden), bf),
+            pltpu.VMEM((chunks, size, wide), jnp.float32),
+            pltpu.VMEM((chunks, size, wide), bf),
+            pltpu.VMEM((chunks, size, wide), bf),
+            pltpu.VMEM((chunks, size, wide), bf),
             dma((owners,)), dma((owners,)),
             dma((2, owners)), dma((2, owners)),
             dma((owners,)), dma((owners,)),
             dma((chunks, 2 * steps)), dma((chunks, 2 * steps)),
             dma((chunks + 2,)),
+            dma((7,)),
         ],
         compiler_params=pltpu.CompilerParams(
             collective_id=0, has_side_effects=True, vmem_limit_bytes=60 * MIB
         ),
     )(features, history, weights, edge_weights, valid, req, cotangent)
 
-    parts = 8
+    parts = 4
     table_rows = hist_rows // parts
     grad_rows = layers * hidden // parts
     out_grads, table, out = pl.pallas_call(
@@ -410,7 +447,7 @@
             pl.BlockSpec((1, table_rows, hidden), lambda i: (0, i, 0)),
             pl.BlockSpec((batch // parts, hidden), lambda i: (i, 0)),
         ),
-        compiler_params=pltpu.CompilerParams(vmem_limit_bytes=32 * MIB),
+        compiler_params=pltpu.CompilerParams(vmem_limit_bytes=60 * MIB),
     )(grads, incoming, history, push_slots, result)
     return out, table, out_grads.reshape(layers, hidden, hidden)
 

time: 141 us -> 120 us (0.85)
  Pallas kernels: 131 us -> 116 us
  local copies, waits for them, and re-layouts: 8.36 us -> 1.54 us
    pallas_call x1, Pallas kernels: 125 us -> 107 us  [body(): pl.pallas_call(functools.partial(step_kernel, owners, slots, grad_scale),...]
    unnamed x10 -> x0, local copies, waits for them, and re-layouts: 6.82 us -> none
    pallas_call x1, Pallas kernels: 5.98 us -> 8.7 us  [body(): pl.pallas_call(finish_kernel, grid=(parts,), out_shape=(jax.ShapeDtypeStr...]
where the time goes in v2:
time: 120 us; the launch traced here: 119 us
  Pallas kernels  116 us (97%)
  local copies, waits for them, and re-layouts  1.54 us (1%)
  other arithmetic  1.32 us (1%)
    pallas_call x1, Pallas kernels, body(): pl.pallas_call(functools.partial(step_kernel, owners, slots, grad_scale),...  107 us
    pallas_call x1, Pallas kernels, body(): pl.pallas_call(finish_kernel, grid=(parts,), out_shape=(jax.ShapeDtypeStr...  8.7 us

profile of v2, /device:TPU:1, one launch (start us, length us, event | category | flops | bytes accessed | tf_op | source)
XLA Modules:
  0.0 119.5 jit_solution(17878110980426429518)
XLA Ops:
  0.6 0.7 iota_compare_fusion
  1.4 0.1 convert_element_type.12
  1.4 0.6 pad_convert_fusion.valid
  2.0 1.5 %broadcast_in_dim.10.req = s32[16,16,128]{2,1,0:T(8,128)} broadcast(s32[16,16]{1,0:T(8,128)} %bitcast.3), dimensions={0,1} | broadcast | bytes 132096 | tf_op jit(solution)/shard_map/broadcast_in_dim | solution.py:378
  3.5 107.3 %shard_map.103 = (bf16[2048,1024]{1,0:T(8,128)(2,1)}, bf16[512,1024]{1,0:T(8,128)(2,1)}, bf16[512,1024]{1,0:T(8,128)(2,1)}) custom-call(bf16[512,1024]{1,0:T(8,128)(2,1)} %feat_in.1, bf16[2,1024,1024]{2,1,0:T(8,128)(2,1)} %hist.1, bf16[2,1024,1024]{2,1,0:T(8,128)(2,1)} %weights_in.1, f32[512,768]{1,0:T(8,128)} %edge_in.1, f32[1,768]{1,0:T(1,128)} %pad_convert_fusion.valid, ...), custom_call_target="tpu_custom_call" | custom-call | tf_op jit(solution)/shard_map/pallas_call | solution.py:385
  110.8 8.7 %shard_map.104 = (f32[2048,1024]{1,0:T(8,128)}, bf16[1,1024,1024]{2,1,0:T(8,128)(2,1)}, bf16[512,1024]{1,0:T(8,128)(2,1)}) custom-call(bf16[2048,1024]{1,0:T(8,128)(2,1)} %get-tuple-element.9.grads, bf16[512,1024]{1,0:T(8,128)(2,1)} %get-tuple-element.10.incoming, bf16[2,1024,1024]{2,1,0:T(8,128)(2,1)} %hist.1, s32[1,512]{1,0:T(1,128)} %slots.1, ...), custom_call_target="tpu_custom_call" | custom-call | tf_op jit(solution)/shard_map/pallas_call | solution.py:430

commit v3 on v2

--- a/solution.py
+++ b/solution.py
@@ -133,6 +133,7 @@
     serve(0)
     each_peer(lambda p: pull_copy(0, p).start())
     serve(1)
+    each_peer(lambda p: pull_copy(1, p).start())
 
     def push_copy(p):
         peer = lax.rem(me + p, owners)
@@ -156,9 +157,7 @@
 
         lax.fori_loop(0, blocks, own_sum, 0)
         each_peer(lambda p, layer_no=layer_no: pull_copy(layer_no, p).wait())
-        if layer_no == 0:
-            each_peer(lambda p: pull_copy(1, p).start())
-        else:
+        if layer_no == 1:
             each_peer(lambda p: push_copy(p).start())
 
         def far_sum(j, c, layer_no=layer_no):

time: 120 us -> 119 us (level)
  no operation moved by 1% of the time
where the time goes in v3:
time: 119 us
  Pallas kernels  115 us (97%)
  local copies, waits for them, and re-layouts  1.54 us (1%)
  other arithmetic  1.32 us (1%)
    pallas_call x1, Pallas kernels, body(): pl.pallas_call(functools.partial(step_kernel, owners, slots, grad_scale),...  107 us
    pallas_call x1, Pallas kernels, body(): pl.pallas_call(finish_kernel, grid=(parts,), out_shape=(jax.ShapeDtypeStr...  8.7 us

profile of v3, /device:TPU:1, one launch (start us, length us, event | category | flops | bytes accessed | tf_op | source)
XLA Modules:
  0.0 118.8 jit_solution(15027256941796270922)
XLA Ops:
  0.6 0.7 iota_compare_fusion
  1.4 0.1 convert_element_type.12
  1.4 0.6 pad_convert_fusion.valid
  2.0 1.5 %broadcast_in_dim.10.req = s32[16,16,128]{2,1,0:T(8,128)} broadcast(s32[16,16]{1,0:T(8,128)} %bitcast.3), dimensions={0,1} | broadcast | bytes 132096 | tf_op jit(solution)/shard_map/broadcast_in_dim | solution.py:377
  3.5 106.6 %shard_map.103 = (bf16[2048,1024]{1,0:T(8,128)(2,1)}, bf16[512,1024]{1,0:T(8,128)(2,1)}, bf16[512,1024]{1,0:T(8,128)(2,1)}) custom-call(bf16[512,1024]{1,0:T(8,128)(2,1)} %feat_in.1, bf16[2,1024,1024]{2,1,0:T(8,128)(2,1)} %hist.1, bf16[2,1024,1024]{2,1,0:T(8,128)(2,1)} %weights_in.1, f32[512,768]{1,0:T(8,128)} %edge_in.1, f32[1,768]{1,0:T(1,128)} %pad_convert_fusion.valid, ...), custom_call_target="tpu_custom_call" | custom-call | tf_op jit(solution)/shard_map/pallas_call | solution.py:384
  110.1 8.7 %shard_map.104 = (f32[2048,1024]{1,0:T(8,128)}, bf16[1,1024,1024]{2,1,0:T(8,128)(2,1)}, bf16[512,1024]{1,0:T(8,128)(2,1)}) custom-call(bf16[2048,1024]{1,0:T(8,128)(2,1)} %get-tuple-element.9.grads, bf16[512,1024]{1,0:T(8,128)(2,1)} %get-tuple-element.10.incoming, bf16[2,1024,1024]{2,1,0:T(8,128)(2,1)} %hist.1, s32[1,512]{1,0:T(1,128)} %slots.1, ...), custom_call_target="tpu_custom_call" | custom-call | tf_op jit(solution)/shard_map/pallas_call | solution.py:429
